TPU v7x, 32 devices: a whole 2x2x4 slice. The times are simulated.
32 devices in a mesh: gx: 2 (over x), gy: 4 (over y, core), gz: 4 (over z).
Axes of the slice: x: 2, y: 2, z: 4, core: 2. Of those that a mesh axis runs over, the one named last changes fastest.
Arguments:
- source: float32 [32, 32, 512], P('gx', 'gy', 'gz'), may hold values from -4.9 to 5.1
- conductivity: float32 [32, 32, 512], P('gx', 'gy', 'gz'), may hold values from 1 to 10
- block_owner: int32 [2, 4, 4], replicated, may hold values from 0 to 15, as said below
Outputs:
- solution: float32 [32, 32, 512], P('gx', 'gy', 'gz')
- residual: float32 [32, 32, 512], P('gx', 'gy', 'gz')
Inputs may be any that keep to these rules, and one draw needn't show every extreme that they name: `block_owner`: every aggregate 0 to 15 holds at least one block.
All inputs are finite; a program needn't handle non-finite values.
Results may differ from a plain program's by a relative error of at most 0.0003.
Values sent between devices are 32-bit elements; how exact they have to be, the bound alone decides.
A program may use at most 64 MiB of HBM per device.

v0:
```python
import jax
import jax.numpy as jnp
from jax import lax
from jax.sharding import PartitionSpec as P

GROUPS = 16
SWEEPS = 2
CYCLES = 2


def padded_2(array, sides, width):
    for axis, dim in sides:
        size, length = (lax.axis_size(axis), array.shape[dim])
        up = [(i, (i + 1) % size) for i in range(size - 1)]
        down = [(j, i) for i, j in up]
        last = lax.slice_in_dim(array, length - width, length, axis=dim)
        leading = lax.slice_in_dim(array, 0, width, axis=dim)
        before = lax.ppermute(last, axis, up)
        after = lax.ppermute(leading, axis, down)
        array = jnp.concatenate([before, array, after], axis=dim)
    return array


def face_terms(padded, multiplier):
    face_x = multiplier * (0.5 * (padded[:-1, 1:-1, 1:-1] + padded[1:, 1:-1, 1:-1]))
    face_y = multiplier * (0.5 * (padded[1:-1, :-1, 1:-1] + padded[1:-1, 1:, 1:-1]))
    face_z = multiplier * (0.5 * (padded[1:-1, 1:-1, :-1] + padded[1:-1, 1:-1, 1:]))
    diagonal = (
        face_x[:-1]
        + face_x[1:]
        + face_y[:, :-1]
        + face_y[:, 1:]
        + face_z[:, :, :-1]
        + face_z[:, :, 1:]
    )
    return (face_x, face_y, face_z, diagonal)


def stencil(padded, face_x, face_y, face_z, diagonal):
    center = padded[1:-1, 1:-1, 1:-1]
    beside = face_x[1:] * padded[2:, 1:-1, 1:-1] + face_x[:-1] * padded[:-2, 1:-1, 1:-1]
    beside = (
        beside + face_y[:, 1:] * padded[1:-1, 2:, 1:-1] + face_y[:, :-1] * padded[1:-1, :-2, 1:-1]
    )
    beside = (
        beside
        + face_z[:, :, 1:] * padded[1:-1, 1:-1, 2:]
        + face_z[:, :, :-1] * padded[1:-1, 1:-1, :-2]
    )
    return diagonal * center - beside


def coarsen(values):
    extent_x, extent_y, extent_z = values.shape
    return values.reshape(extent_x // 2, 2, extent_y // 2, 2, extent_z // 2, 2).sum(axis=(1, 3, 5))


def refine(values):
    extent_x, extent_y, extent_z = values.shape
    spread = jnp.broadcast_to(
        values[:, None, :, None, :, None], (extent_x, 2, extent_y, 2, extent_z, 2)
    )
    return spread.reshape(2 * extent_x, 2 * extent_y, 2 * extent_z)


def smooth_sweeps(values, target, coeffs, padder, repeats):
    for sweep_index in range(repeats):
        values = values + 0.8 * (target - stencil(padder(values), *coeffs)) / coeffs[3]
    return values


def edge_copy(values, axis_dim, at_first, at_last):
    length = values.shape[axis_dim]
    low_part = lax.slice_in_dim(values, 0, 1, axis=axis_dim)
    low_edge = lax.slice_in_dim(values, 1, 2, axis=axis_dim)
    high_part = lax.slice_in_dim(values, length - 1, length, axis=axis_dim)
    high_edge = lax.slice_in_dim(values, length - 2, length - 1, axis=axis_dim)
    middle_part = lax.slice_in_dim(values, 1, length - 1, axis=axis_dim)
    low_part = jnp.where(at_first, low_edge, low_part)
    high_part = jnp.where(at_last, high_edge, high_part)
    return jnp.concatenate([low_part, middle_part, high_part], axis=axis_dim)


def on_device(source, conductivity, block_owner):
    highest = lax.Precision.HIGHEST
    index_x, index_y, index_z = (lax.axis_index("gx"), lax.axis_index("gy"), lax.axis_index("gz"))
    size_x, size_y, size_z = (lax.axis_size("gx"), lax.axis_size("gy"), lax.axis_size("gz"))
    at_low = (index_x == 0, index_y == 0, index_z == 0)
    at_high = (index_x == size_x - 1, index_y == size_y - 1, index_z == size_z - 1)
    labels = jnp.arange(GROUPS, dtype=jnp.int32)

    def edge_fill(padded):
        for axis_dim in range(3):
            padded = edge_copy(padded, axis_dim, at_low[axis_dim], at_high[axis_dim])
        return padded

    finest = face_terms(
        edge_fill(padded_2(conductivity, (("gx", 0), ("gy", 1), ("gz", 2)), 1)), 1.0
    )
    middle_k = coarsen(conductivity) * 0.125
    middle = face_terms(edge_fill(padded_2(middle_k, (("gx", 0), ("gy", 1), ("gz", 2)), 1)), 2.0)
    coarse_k = coarsen(middle_k) * 0.125

    def fine_padder(values):
        return padded_2(values, (("gx", 0), ("gy", 1), ("gz", 2)), 1)

    def middle_padder(values):
        return padded_2(values, (("gx", 0), ("gy", 1), ("gz", 2)), 1)

    part_x, part_y, part_z = coarse_k.shape

    def assemble(stacked):
        grouped = stacked.reshape(size_x, size_y, part_x, part_y, part_z).transpose(0, 2, 1, 3, 4)
        return grouped.reshape(size_x * part_x, size_y * part_y, part_z)

    slab_k = assemble(lax.all_gather(coarse_k[None], ("gx", "gy"), axis=0, tiled=True))
    slab_k = padded_2(slab_k, (("gz", 2),), 1)
    slab_k = edge_copy(slab_k, 2, at_low[2], at_high[2])
    slab_k = jnp.pad(slab_k, ((1, 1), (1, 1), (0, 0)), mode="edge")
    coarse = face_terms(slab_k, 4.0)
    face_x, face_y, face_z, _ = coarse
    member = (block_owner[:, :, index_z][..., None] == labels).astype(jnp.float32)
    member_above = (
        block_owner[:, :, jnp.minimum(index_z + 1, size_z - 1)][..., None] == labels
    ).astype(jnp.float32)
    plane_x = face_x[::part_x].reshape(size_x + 1, size_y, part_y, part_z).sum(axis=(2, 3))
    plane_y = face_y[:, ::part_y].reshape(size_x, part_x, size_y + 1, part_z).sum(axis=(1, 3))
    lower_z = face_z[:, :, 0].reshape(size_x, part_x, size_y, part_y).sum(axis=(1, 3))
    upper_z = face_z[:, :, -1].reshape(size_x, part_x, size_y, part_y).sum(axis=(1, 3))
    outward = plane_x[:-1] + plane_x[1:] + plane_y[:, :-1] + plane_y[:, 1:] + lower_z + upper_z
    system = jnp.einsum("abg,ab,abh->gh", member, outward, member, precision=highest)
    coupled = jnp.einsum(
        "abg,ab,abh->gh", member[:-1], plane_x[1:-1], member[1:], precision=highest
    )
    coupled = coupled + jnp.einsum(
        "abg,ab,abh->gh", member[:, :-1], plane_y[:, 1:-1], member[:, 1:], precision=highest
    )
    coupled = coupled + jnp.einsum(
        "abg,ab,abh->gh",
        member,
        jnp.where(index_z < size_z - 1, upper_z, 0.0),
        member_above,
        precision=highest,
    )
    factor = jnp.linalg.cholesky(lax.psum(system - coupled - coupled.T, "gz"))

    def slab_padder(values):
        rimmed = padded_2(values, (("gz", 2),), 1)
        return jnp.pad(rimmed, ((1, 1), (1, 1), (0, 0)))

    solution = jnp.zeros_like(source)
    for cycle_index in range(CYCLES):
        solution = smooth_sweeps(solution, source, finest, fine_padder, SWEEPS)
        level_rhs = coarsen(source - stencil(fine_padder(solution), *finest))
        level_one = smooth_sweeps(
            jnp.zeros_like(level_rhs), level_rhs, middle, middle_padder, SWEEPS
        )
        next_rhs = coarsen(level_rhs - stencil(middle_padder(level_one), *middle))
        slab_rhs = assemble(lax.all_gather(next_rhs[None], ("gx", "gy"), axis=0, tiled=True))
        level_two = smooth_sweeps(jnp.zeros_like(slab_rhs), slab_rhs, coarse, slab_padder, SWEEPS)
        remain = slab_rhs - stencil(slab_padder(level_two), *coarse)
        block_sums = remain.reshape(size_x, part_x, size_y, part_y, part_z).sum(axis=(1, 3, 4))
        group_rhs = lax.psum(jnp.einsum("abg,ab->g", member, block_sums, precision=highest), "gz")
        coarse_sol = jax.scipy.linalg.cho_solve((factor, True), group_rhs)
        lifted = jnp.einsum("abg,g->ab", member, coarse_sol, precision=highest)
        level_two = (
            level_two.reshape(size_x, part_x, size_y, part_y, part_z)
            + lifted[:, None, :, None, None]
        ).reshape(level_two.shape)
        level_two = smooth_sweeps(level_two, slab_rhs, coarse, slab_padder, SWEEPS)
        level_one = level_one + refine(
            lax.dynamic_slice(
                level_two, (index_x * part_x, index_y * part_y, 0), (part_x, part_y, part_z)
            )
        )
        level_one = smooth_sweeps(level_one, level_rhs, middle, middle_padder, SWEEPS)
        solution = solution + refine(level_one)
        solution = smooth_sweeps(solution, source, finest, fine_padder, SWEEPS)
    residual = source - stencil(fine_padder(solution), *finest)
    return (solution, residual)


def solution(mesh):
    in_specs = (P("gx", "gy", "gz"), P("gx", "gy", "gz"), P())
    out_specs = (P("gx", "gy", "gz"), P("gx", "gy", "gz"))
    return jax.shard_map(
        on_device, mesh=mesh, in_specs=in_specs, out_specs=out_specs, check_vma=False
    )
```

profile of v0, /device:TPU:0, one launch (start us, length us, event | category | flops | bytes accessed | tf_op | source)
XLA Modules:
  0.0 665.7 jit_solution(18075115751939105788)
XLA Ops:
  2.1 4.8 collective-permute-start.7
  6.9 6.3 reshape.113
  17.8 10.2 %all-gather.1 = f32[32,2,32]{2,1,0:T(2,128)S(1)} all-gather(f32[4,2,32]{2,1,0:T(2,128)S(1)} %copy.77), channel_id=3, replica_groups=mesh['gx'=2,'gy'=4,'gz'=4] {'gx','gy'}, dimensions={0}, use_global_device_ids=true | all-gather | bytes 9216 | tf_op jit(solution)/shard_map/all_gather | solution.py:116
  119.3 5.0 collective-permute-start.17
  141.9 5.0 collective-permute-start.23
  153.7 5.6 reshape.112
  195.9 5.0 collective-permute-start.47
  203.4 12.6 %all-gather = f32[32,2,32]{2,1,0:T(2,128)S(1)} all-gather(f32[4,2,32]{2,1,0:T(2,128)S(1)} %copy.73), channel_id=2, replica_groups=mesh['gx'=2,'gy'=4,'gz'=4] {'gx','gy'}, dimensions={0}, use_global_device_ids=true | all-gather | bytes 9216 | tf_op jit(solution)/shard_map/all_gather | solution.py:159
  237.3 10.7 %all-reduce.15 = (f32[16,16]{0,1:T(8,128)S(1)}, f32[16]{0:T(128)S(1)}) all-reduce(f32[16,16]{0,1:T(8,128)S(1)} %bitcast_subtract_fusion, f32[16]{0:T(128)S(1)} %convolution_bitcast_fusion.4), channel_id=1, replica_groups=mesh['gx'=2,'gy'=4,'gz'=4] {'gz'}, use_global_device_ids=true, to_apply=%region_10.11 | all-reduce | flops 272 | bytes 2176 | tf_op jit(solution)/shard_map/psum | solution.py:145
  303.4 5.0 collective-permute-start.71
  347.2 5.1 collective-permute-start.81
  354.5 4.7 collective-permute-start.83
  370.6 5.1 collective-permute-start.87
  394.0 5.1 collective-permute-start.93
  417.4 5.1 collective-permute-start.99
  432.3 5.6 reshape.124
  449.0 5.1 collective-permute-start.105
  471.2 5.1 collective-permute-start.111
  478.5 4.8 collective-permute-start.113
  485.6 14.5 %all-gather.2 = f32[32,2,32]{2,1,0:T(2,128)S(1)} all-gather(f32[4,2,32]{2,1,0:T(2,128)S(1)} %copy.94), channel_id=4, replica_groups=mesh['gx'=2,'gy'=4,'gz'=4] {'gx','gy'}, dimensions={0}, use_global_device_ids=true | all-gather | bytes 9216 | tf_op jit(solution)/shard_map/all_gather | solution.py:159
  521.2 10.4 %psum.23 = f32[16]{0:T(128)S(1)} all-reduce(f32[16]{0:T(128)S(1)} %convolution_bitcast_fusion.3), channel_id=1, replica_groups=mesh['gx'=2,'gy'=4,'gz'=4] {'gz'}, use_global_device_ids=true, to_apply=%region_20.22 | all-reduce | flops 16 | bytes 128 | tf_op jit(solution)/shard_map/psum | solution.py:163
  582.9 5.0 collective-permute-start.133
  626.7 5.1 collective-permute-start.143
  650.1 5.1 collective-permute-start.149
  (573 shorter events, 506.3 us)
Async XLA Ops:
  0.7 76.3 %collective-permute-start.6 = (f32[1,8,128]{2,1,0:T(8,128)S(1)}, f32[1,8,128]{2,1,0:T(8,128)S(1)}, u32[]{:S(2)}, u32[]{:S(2)}) collective-permute-start(f32[1,8,128]{2,1,0:T(8,128)S(1)} %broadcast.153), channel_id=1, source_target_pairs={{16,0},{17,1},{18,2},{19,3},{20,4},{21,5},{22,6},{23,7},{24,8},{25... | collective-permute-start | bytes 12296 | tf_op jit(solution)/shard_map/ppermute | solution.py:19
  2.1 76.2 %collective-permute-start.7 = (f32[1,8,128]{2,1,0:T(8,128)S(1)}, f32[1,8,128]{2,1,0:T(8,128)S(1)}, u32[]{:S(2)}, u32[]{:S(2)}) collective-permute-start(f32[1,8,128]{2,1,0:T(8,128)S(1)} %broadcast.153), channel_id=1, source_target_pairs={{0,16},{1,17},{2,18},{3,19},{4,20},{5,21},{6,22},{7,23},{8,24},{9,... | collective-permute-start | bytes 12296 | tf_op jit(solution)/shard_map/ppermute | solution.py:18
  15.8 24.7 %collective-permute-start.24 = (f32[1,4,64]{2,1,0:T(4,128)S(1)}, f32[1,4,64]{2,1,0:T(4,128)S(1)}, u32[]{:S(2)}, u32[]{:S(2)}) collective-permute-start(f32[1,4,64]{2,1,0:T(4,128)S(1)} %get-tuple-element.174), channel_id=1, source_target_pairs={{0,16},{1,17},{2,18},{3,19},{4,20},{5,21},{6,22},{7,23},{8,24},{9,... | collective-permute-start | bytes 3080 | tf_op jit(solution)/shard_map/ppermute | solution.py:18
  33.3 11.8 %collective-permute-start.25 = (f32[1,4,64]{2,1,0:T(4,128)S(1)}, f32[1,4,64]{2,1,0:T(4,128)S(1)}, u32[]{:S(2)}, u32[]{:S(2)}) collective-permute-start(f32[1,4,64]{2,1,0:T(4,128)S(1)} %get-tuple-element.175), channel_id=1, source_target_pairs={{16,0},{17,1},{18,2},{19,3},{20,4},{21,5},{22,6},{23,7},{24,8},{25... | collective-permute-start | bytes 3080 | tf_op jit(solution)/shard_map/ppermute | solution.py:19
  37.5 11.2 %collective-permute-start.30 = (f32[1,4,64]{2,1,0:T(4,128)S(1)}, f32[1,4,64]{2,1,0:T(4,128)S(1)}, u32[]{:S(2)}, u32[]{:S(2)}) collective-permute-start(f32[1,4,64]{2,1,0:T(4,128)S(1)} %broadcast.156), channel_id=1, source_target_pairs={{16,0},{17,1},{18,2},{19,3},{20,4},{21,5},{22,6},{23,7},{24,8},{25... | collective-permute-start | bytes 3080 | tf_op jit(solution)/shard_map/ppermute | solution.py:19
  40.6 9.4 %collective-permute-start.31 = (f32[1,4,64]{2,1,0:T(4,128)S(1)}, f32[1,4,64]{2,1,0:T(4,128)S(1)}, u32[]{:S(2)}, u32[]{:S(2)}) collective-permute-start(f32[1,4,64]{2,1,0:T(4,128)S(1)} %broadcast.156), channel_id=1, source_target_pairs={{0,16},{1,17},{2,18},{3,19},{4,20},{5,21},{6,22},{7,23},{8,24},{9,... | collective-permute-start | bytes 3080 | tf_op jit(solution)/shard_map/ppermute | solution.py:18
  45.1 155.8 %collective-permute-start.50 = (f32[8,8,1]{2,1,0:T(8,128)S(1)}, f32[8,8,1]{2,1,0:T(8,128)S(1)}, u32[]{:S(2)}, u32[]{:S(2)}) collective-permute-start(f32[8,8,1]{2,1,0:T(8,128)S(1)} %broadcast.158), channel_id=1, source_target_pairs={{0,1},{1,2},{2,3},{4,5},{5,6},{6,7},{8,9},{9,10},{10,11},{12,13},{... | collective-permute-start | bytes 776 | tf_op jit(solution)/shard_map/ppermute | solution.py:18
  53.8 7.9 %collective-permute-start.33 = (f32[10,1,64]{2,1,0:T(1,128)S(1)}, f32[10,1,64]{2,1,0:T(1,128)S(1)}, u32[]{:S(2)}, u32[]{:S(2)}) collective-permute-start(f32[10,1,64]{2,1,0:T(1,128)S(1)} %get-tuple-element.154), channel_id=1, source_target_pairs={{0,4},{4,8},{8,12},{1,5},{5,9},{9,13},{2,6},{6,10},{10,14},{3,7},{... | collective-permute-start | bytes 7688 | tf_op jit(solution)/shard_map/ppermute | solution.py:18
  63.3 137.6 %collective-permute-start.51 = (f32[8,8,1]{2,1,0:T(8,128)S(1)}, f32[8,8,1]{2,1,0:T(8,128)S(1)}, u32[]{:S(2)}, u32[]{:S(2)}) collective-permute-start(f32[8,8,1]{2,1,0:T(8,128)S(1)} %broadcast.158), channel_id=1, source_target_pairs={{1,0},{2,1},{3,2},{5,4},{6,5},{7,6},{9,8},{10,9},{11,10},{13,12},{... | collective-permute-start | bytes 776 | tf_op jit(solution)/shard_map/ppermute | solution.py:19
  75.6 86.2 %collective-permute-start.34 = (f32[10,6,1]{2,1,0:T(8,128)S(1)}, f32[10,6,1]{2,1,0:T(8,128)S(1)}, u32[]{:S(2)}, u32[]{:S(2)}) collective-permute-start(f32[10,6,1]{2,1,0:T(8,128)S(1)} %get-tuple-element.108), channel_id=1, source_target_pairs={{1,0},{2,1},{3,2},{5,4},{6,5},{7,6},{9,8},{10,9},{11,10},{13,12},{... | collective-permute-start | bytes 728 | tf_op jit(solution)/shard_map/ppermute | solution.py:19
  79.6 7.8 %collective-permute-start.8 = (f32[18,1,128]{2,1,0:T(1,128)S(1)}, f32[18,1,128]{2,1,0:T(1,128)S(1)}, u32[]{:S(2)}, u32[]{:S(2)}) collective-permute-start(f32[18,1,128]{2,1,0:T(1,128)S(1)} %get-tuple-element.65), channel_id=1, source_target_pairs={{4,0},{8,4},{12,8},{5,1},{9,5},{13,9},{6,2},{10,6},{14,10},{7,3},{... | collective-permute-start | bytes 27656 | tf_op jit(solution)/shard_map/ppermute | solution.py:19
  82.9 9.0 %collective-permute-start.9 = (f32[18,1,128]{2,1,0:T(1,128)S(1)}, f32[18,1,128]{2,1,0:T(1,128)S(1)}, u32[]{:S(2)}, u32[]{:S(2)}) collective-permute-start(f32[18,1,128]{2,1,0:T(1,128)S(1)} %get-tuple-element.64), channel_id=1, source_target_pairs={{0,4},{4,8},{8,12},{1,5},{5,9},{9,13},{2,6},{6,10},{10,14},{3,7},{... | collective-permute-start | bytes 27656 | tf_op jit(solution)/shard_map/ppermute | solution.py:18
  87.4 8.5 %collective-permute-start.4 = (f32[18,10,1]{2,1,0:T(8,128)S(1)}, f32[18,10,1]{2,1,0:T(8,128)S(1)}, u32[]{:S(2)}, u32[]{:S(2)}) collective-permute-start(f32[18,10,1]{2,1,0:T(8,128)S(1)} %get-tuple-element.36), channel_id=1, source_target_pairs={{0,1},{1,2},{2,3},{4,5},{5,6},{6,7},{8,9},{9,10},{10,11},{12,13},{... | collective-permute-start | bytes 2168 | tf_op jit(solution)/shard_map/ppermute | solution.py:18
  92.0 8.1 %collective-permute-start.5 = (f32[18,10,1]{2,1,0:T(8,128)S(1)}, f32[18,10,1]{2,1,0:T(8,128)S(1)}, u32[]{:S(2)}, u32[]{:S(2)}) collective-permute-start(f32[18,10,1]{2,1,0:T(8,128)S(1)} %get-tuple-element.37), channel_id=1, source_target_pairs={{1,0},{2,1},{3,2},{5,4},{6,5},{7,6},{9,8},{10,9},{11,10},{13,12},{... | collective-permute-start | bytes 2168 | tf_op jit(solution)/shard_map/ppermute | solution.py:19
  95.9 8.2 %collective-permute-start.10 = (f32[18,10,1]{2,1,0:T(8,128)S(1)}, f32[18,10,1]{2,1,0:T(8,128)S(1)}, u32[]{:S(2)}, u32[]{:S(2)}) collective-permute-start(f32[18,10,1]{2,1,0:T(8,128)S(1)} %get-tuple-element.38), channel_id=1, source_target_pairs={{1,0},{2,1},{3,2},{5,4},{6,5},{7,6},{9,8},{10,9},{11,10},{13,12},{... | collective-permute-start | bytes 2168 | tf_op jit(solution)/shard_map/ppermute | solution.py:19
  118.0 8.7 %collective-permute-start.16 = (f32[18,10,1]{2,1,0:T(8,128)S(1)}, f32[18,10,1]{2,1,0:T(8,128)S(1)}, u32[]{:S(2)}, u32[]{:S(2)}) collective-permute-start(f32[18,10,1]{2,1,0:T(8,128)S(1)} %get-tuple-element.34), channel_id=1, source_target_pairs={{1,0},{2,1},{3,2},{5,4},{6,5},{7,6},{9,8},{10,9},{11,10},{13,12},{... | collective-permute-start | bytes 2168 | tf_op jit(solution)/shard_map/ppermute | solution.py:19
  119.3 8.6 %collective-permute-start.17 = (f32[18,10,1]{2,1,0:T(8,128)S(1)}, f32[18,10,1]{2,1,0:T(8,128)S(1)}, u32[]{:S(2)}, u32[]{:S(2)}) collective-permute-start(f32[18,10,1]{2,1,0:T(8,128)S(1)} %get-tuple-element.35), channel_id=1, source_target_pairs={{0,1},{1,2},{2,3},{4,5},{5,6},{6,7},{8,9},{9,10},{10,11},{12,13},{... | collective-permute-start | bytes 2168 | tf_op jit(solution)/shard_map/ppermute | solution.py:18
  140.6 9.0 %collective-permute-start.22 = (f32[18,10,1]{2,1,0:T(8,128)S(1)}, f32[18,10,1]{2,1,0:T(8,128)S(1)}, u32[]{:S(2)}, u32[]{:S(2)}) collective-permute-start(f32[18,10,1]{2,1,0:T(8,128)S(1)} %get-tuple-element.32), channel_id=1, source_target_pairs={{1,0},{2,1},{3,2},{5,4},{6,5},{7,6},{9,8},{10,9},{11,10},{13,12},{... | collective-permute-start | bytes 2168 | tf_op jit(solution)/shard_map/ppermute | solution.py:19
  141.9 11.6 %collective-permute-start.23 = (f32[18,10,1]{2,1,0:T(8,128)S(1)}, f32[18,10,1]{2,1,0:T(8,128)S(1)}, u32[]{:S(2)}, u32[]{:S(2)}) collective-permute-start(f32[18,10,1]{2,1,0:T(8,128)S(1)} %get-tuple-element.33), channel_id=1, source_target_pairs={{0,1},{1,2},{2,3},{4,5},{5,6},{6,7},{8,9},{9,10},{10,11},{12,13},{... | collective-permute-start | bytes 2168 | tf_op jit(solution)/shard_map/ppermute | solution.py:18
  149.5 12.3 %collective-permute-start.35 = (f32[10,6,1]{2,1,0:T(8,128)S(1)}, f32[10,6,1]{2,1,0:T(8,128)S(1)}, u32[]{:S(2)}, u32[]{:S(2)}) collective-permute-start(f32[10,6,1]{2,1,0:T(8,128)S(1)} %get-tuple-element.109), channel_id=1, source_target_pairs={{0,1},{1,2},{2,3},{4,5},{5,6},{6,7},{8,9},{9,10},{10,11},{12,13},{... | collective-permute-start | bytes 728 | tf_op jit(solution)/shard_map/ppermute | solution.py:18
  354.5 7.4 %collective-permute-start.83 = (f32[18,10,1]{2,1,0:T(8,128)S(1)}, f32[18,10,1]{2,1,0:T(8,128)S(1)}, u32[]{:S(2)}, u32[]{:S(2)}) collective-permute-start(f32[18,10,1]{2,1,0:T(8,128)S(1)} %get-tuple-element.29), channel_id=1, source_target_pairs={{0,1},{1,2},{2,3},{4,5},{5,6},{6,7},{8,9},{9,10},{10,11},{12,13},{... | collective-permute-start | bytes 2168 | tf_op jit(solution)/shard_map/ppermute | solution.py:18
  377.9 7.4 %collective-permute-start.89 = (f32[18,10,1]{2,1,0:T(8,128)S(1)}, f32[18,10,1]{2,1,0:T(8,128)S(1)}, u32[]{:S(2)}, u32[]{:S(2)}) collective-permute-start(f32[18,10,1]{2,1,0:T(8,128)S(1)} %get-tuple-element.27), channel_id=1, source_target_pairs={{0,1},{1,2},{2,3},{4,5},{5,6},{6,7},{8,9},{9,10},{10,11},{12,13},{... | collective-permute-start | bytes 2168 | tf_op jit(solution)/shard_map/ppermute | solution.py:18
  401.3 7.4 %collective-permute-start.95 = (f32[18,10,1]{2,1,0:T(8,128)S(1)}, f32[18,10,1]{2,1,0:T(8,128)S(1)}, u32[]{:S(2)}, u32[]{:S(2)}) collective-permute-start(f32[18,10,1]{2,1,0:T(8,128)S(1)} %get-tuple-element.25), channel_id=1, source_target_pairs={{0,1},{1,2},{2,3},{4,5},{5,6},{6,7},{8,9},{9,10},{10,11},{12,13},{... | collective-permute-start | bytes 2168 | tf_op jit(solution)/shard_map/ppermute | solution.py:18
  424.7 7.4 %collective-permute-start.101 = (f32[18,10,1]{2,1,0:T(8,128)S(1)}, f32[18,10,1]{2,1,0:T(8,128)S(1)}, u32[]{:S(2)}, u32[]{:S(2)}) collective-permute-start(f32[18,10,1]{2,1,0:T(8,128)S(1)} %get-tuple-element.23), channel_id=1, source_target_pairs={{0,1},{1,2},{2,3},{4,5},{5,6},{6,7},{8,9},{9,10},{10,11},{12,13},{... | collective-permute-start | bytes 2168 | tf_op jit(solution)/shard_map/ppermute | solution.py:18
  (132 other events, 846.1 us)
where the time goes:
time: 676 us; the launch traced here: 666 us
  starting transfers between devices  406 us (60%)
  waiting for transfers between devices  134 us (20%)
  blocking collectives  58.4 us (9%)
  local copies, waits for them, and re-layouts  39.1 us (6%)
  other arithmetic  22.6 us (3%)
    ppermute x76, starting transfers between devices, padded_2(): before = lax.ppermute(last, axis, up)  308 us
    ppermute x76, starting transfers between devices, padded_2(): after = lax.ppermute(leading, axis, down)  98.2 us
    ppermute x76, waiting for transfers between devices, padded_2(): before = lax.ppermute(last, axis, up)  68.9 us
    ppermute x76, waiting for transfers between devices, padded_2(): after = lax.ppermute(leading, axis, down)  65 us
    all_gather x2, blocking collectives, on_device(): lax.all_gather(next_rhs[None], ('gx', 'gy'), axis=0, tiled=True)  27.1 us
    reshape x5, local copies, waits for them, and re-layouts, coarsen(): values.reshape(extent_x // 2, 2, extent_y // 2, 2, extent_z // 2, 2)  18.5 us
  transfers between devices with their start and end apart: 152, of which 89 were waited for; matrix products, arithmetic and copies ran while one was open for 4% of the time, Pallas kernels for 0%

commit v1 on v0

v1 whole, which is shorter than its diff:
```python
import functools

import jax
import jax.numpy as jnp
from jax import lax
from jax.experimental import pallas as pl
from jax.experimental.pallas import tpu as pltpu
from jax.sharding import PartitionSpec as P

GROUPS = 16
SWEEPS = 2
CYCLES = 2
F32 = jnp.float32
MESH = pl.DeviceIdType.MESH
HIGHEST = lax.Precision.HIGHEST
AXES = ("gx", "gy", "gz")


def iota(shape, dim):
    return lax.broadcasted_iota(jnp.int32, shape, dim)


def own_faces(u):
    nx = u.shape[0]
    lane, plane = iota(u.shape, 2), iota(u.shape, 0)
    z_low = jnp.sum(jnp.where(lane == plane, u[:, :, 0:1], 0.0), axis=0)
    z_high = jnp.sum(jnp.where(lane == plane, u[:, :, 127:128], 0.0), axis=0)
    y_low = [u[x, 0:1, :] for x in range(nx)]
    y_high = [u[x, 7:8, :] for x in range(nx)]
    return [u[0], u[nx - 1], y_low, y_high, z_low, z_high]


def spread_y(rows):
    return jnp.stack([jnp.broadcast_to(row, (8, 128)) for row in rows])


def spread_z(packed, nx):
    return jnp.stack([jnp.broadcast_to(packed[:, x : x + 1], (8, 128)) for x in range(nx)])


def rolled(u, w):
    s, l = iota(u.shape, 1), iota(u.shape, 2)
    gap = jnp.zeros((1, 8, 128), F32)
    return [
        jnp.concatenate([gap, u[:-1]], axis=0),
        jnp.concatenate([u[1:], gap], axis=0),
        jnp.where(s < w, 0.0, pltpu.roll(u, w, 1)),
        jnp.where(s >= 8 - w, 0.0, pltpu.roll(u, 8 - w, 1)),
        jnp.where(l < w, 0.0, pltpu.roll(u, w, 2)),
        jnp.where(l >= 128 - w, 0.0, pltpu.roll(u, 128 - w, 2)),
    ]


def pair_sum(v, w):
    s, l = iota(v.shape, 1), iota(v.shape, 2)
    v = v + jnp.where(s % (2 * w) < w, pltpu.roll(v, 8 - w, 1), pltpu.roll(v, w, 1))
    return v + jnp.where(l % (2 * w) < w, pltpu.roll(v, 128 - w, 2), pltpu.roll(v, w, 2))


def restrict(v, w):
    v = jnp.stack([v[2 * i] + v[2 * i + 1] for i in range(v.shape[0] // 2)])
    return pair_sum(v, w)


def prolong(v):
    return jnp.stack([v[i // 2] for i in range(2 * v.shape[0])])


def coarse_shifts(v, sx, sy, edge):
    s, l = iota(v.shape, 1), iota(v.shape, 2)
    lz = v.shape[2]
    own = v if edge else jnp.zeros_like(v)
    n = sx * sy

    def across_x(r, down):
        if sx == 1:
            return own
        if down:
            return jnp.concatenate([own[:sy], r[: n - sy]], axis=0)
        return jnp.concatenate([r[sy:], own[n - sy :]], axis=0)

    def across_y(r, down):
        parts = []
        for i in range(sx):
            a, b = i * sy, (i + 1) * sy
            inner = [r[a : b - 1]] if down else [r[a + 1 : b]]
            inner = inner if sy > 1 else []
            parts += ([own[a : a + 1]] + inner) if down else (inner + [own[b - 1 : b]])
        return jnp.concatenate(parts, axis=0)

    up2, down2 = pltpu.roll(v, 2, 1), pltpu.roll(v, 6, 1)
    up1, down1 = pltpu.roll(v, 1, 1), pltpu.roll(v, 7, 1)
    return [
        jnp.where(s < 2, across_x(up2, True), up2),
        jnp.where(s >= 6, across_x(down2, False), down2),
        jnp.where(s % 2 == 0, across_y(down1, True), up1),
        jnp.where(s % 2 == 1, across_y(up1, False), down1),
        jnp.where(l == 0, own, pltpu.roll(v, 1, 2)),
        jnp.where(l == lz - 1, own, pltpu.roll(v, lz - 1, 2)),
    ]


def kernel(sizes, source_ref, k_ref, owner_ref, sol_ref, res_ref,
           sbuf, rbuf, gsend, gbuf, c0, c1, c2, member_ref, wide_ref,
           ssem, rsem, gssem, grsem):
    sx, sy, sz = sizes
    count, n_xy, lz = sx * sy * sz, sx * sy, 32 * sz
    me = [lax.axis_index(a) for a in AXES]
    my_xy = me[0] * sy + me[1]
    linear = my_xy * sz + me[2]
    edge = [me[0] == 0, me[0] == sx - 1, me[1] == 0, me[1] == sy - 1, me[2] == 0, me[2] == sz - 1]

    rbuf[...] = jnp.zeros_like(rbuf)

    def coords(d):
        t = lax.rem(linear + d, count)
        return (t // (sy * sz), (t // sz) % sy, t % sz)

    barrier = pltpu.get_barrier_semaphore()

    @pl.loop(1, count)
    def _(d):
        pl.semaphore_signal(barrier, inc=1, device_id=coords(d), device_id_type=MESH)

    pl.semaphore_wait(barrier, count - 1)

    def copy_of(slot, d, nx):
        axis, step = d // 2, 1 if d % 2 else -1
        there = [me[a] + step if a == axis else me[a] for a in range(3)]
        rows = nx if axis == 1 else 8
        return pltpu.make_async_remote_copy(
            src_ref=sbuf.at[slot, d, pl.ds(0, rows)],
            dst_ref=rbuf.at[slot, d ^ 1, pl.ds(0, rows)],
            send_sem=ssem.at[slot, d],
            recv_sem=rsem.at[slot, d ^ 1],
            device_id=tuple(there),
            device_id_type=MESH,
        )

    def send(slot, faces, nx):
        for d in (4, 5, 2, 3, 0, 1):
            if d in (2, 3):
                for x in range(nx):
                    sbuf[slot, d, x : x + 1, :] = faces[d][x]
            else:
                sbuf[slot, d, 0:8, :] = faces[d]

            @pl.when(jnp.logical_not(edge[d]))
            def _():
                copy_of(slot, d, nx).start()

    def receive(slot, nx):
        for d in range(6):
            @pl.when(jnp.logical_not(edge[d]))
            def _():
                copy = copy_of(slot, d, nx)
                copy.wait_send()
                rows = nx if d // 2 == 1 else 8
                pltpu.make_async_copy(
                    rbuf.at[slot, d, pl.ds(0, rows)], rbuf.at[slot, d, pl.ds(0, rows)],
                    rsem.at[slot, d],
                ).wait()

    def got(slot, nx):
        return [
            [rbuf[slot, d, x : x + 1, :] for x in range(nx)] if d in (2, 3)
            else rbuf[slot, d, 0:8, :]
            for d in range(6)
        ]

    lane_base = (me[2] % 4) * 32

    def gather_copy(use, d):
        return pltpu.make_async_remote_copy(
            src_ref=gsend.at[use],
            dst_ref=gbuf.at[use, linear],
            send_sem=gssem.at[use],
            recv_sem=grsem.at[use],
            device_id=coords(d),
            device_id_type=MESH,
        )

    def gather_start(use, v):
        s = iota((8, 128), 0)
        straight = (s % 2) == (s // 4)
        packed = jnp.zeros((8, 128), F32)
        for x in range(4):
            both = jnp.where(straight, v[x], pltpu.roll(v[x], 4, 0))
            packed = jnp.where(s // 2 == x, both, packed)
        pick = (iota((128, 128), 0) == 4 * (iota((128, 128), 1) - lane_base)).astype(F32)
        packed = jnp.dot(packed, pick, precision=HIGHEST, preferred_element_type=F32)
        gsend[use] = packed
        gbuf[use, linear] = packed

        @pl.loop(1, count)
        def _(d):
            gather_copy(use, d).start()

    def gather_wait(use):
        whole = gbuf.at[use, pl.ds(0, count - 1)]
        pltpu.make_async_copy(whole, whole, gssem.at[use]).wait()
        pltpu.make_async_copy(whole, whole, grsem.at[use]).wait()
        rows = []
        for i in range(n_xy):
            parts = []
            for first in range(0, sz, 4):
                part = gbuf[use, i * sz + first]
                for j in range(first + 1, min(first + 4, sz)):
                    part = part + gbuf[use, i * sz + j]
                parts.append(part)
            rows.append(parts[0] if len(parts) == 1 else jnp.concatenate(parts, axis=1))
        return jnp.stack(rows)

    def set_up(c_ref, k, faces, halo, w):
        nx = k.shape[0]
        beside = rolled(k, w)
        shape = k.shape
        p, s, l = iota(shape, 0), iota(shape, 1), iota(shape, 2)
        masks = [p < 1, p >= nx - 1, s < w, s >= 8 - w, l < w, l >= 128 - w]
        total = jnp.zeros(shape, F32)
        for d in range(6):
            if d in (2, 3):
                far = spread_y([jnp.where(edge[d], a, b) for a, b in zip(faces[d], halo[d])])
            else:
                far = jnp.where(edge[d], faces[d], halo[d])
                far = spread_z(far, nx) if d >= 4 else jnp.broadcast_to(far[None], shape)
            c = float(w) * (0.5 * (k + jnp.where(masks[d], far, beside[d])))
            c_ref[d] = c
            total = total + c
        c_ref[6] = total
        c_ref[7] = 0.8 / total

    k0 = k_ref[...]
    k0_faces = own_faces(k0)
    send(0, k0_faces, 16)
    k1 = restrict(k0, 1) * 0.125
    k1_faces = own_faces(k1)
    send(1, k1_faces, 8)
    k2 = restrict(k1, 2) * 0.125
    gather_start(0, k2)

    receive(0, 16)
    set_up(c0, k0, k0_faces, got(0, 16), 1)
    receive(1, 8)
    set_up(c1, k1, k1_faces, got(1, 8), 2)

    phase = [0]

    def residual(c_ref, u, b, w, beside_wait=None):
        nx = u.shape[0]
        slot = 2 + phase[0] % 2
        phase[0] += 1
        send(slot, own_faces(u), nx)
        inner = rolled(u, w)
        r = b - c_ref[6] * u
        for d in range(6):
            r = r + c_ref[d] * inner[d]
        if beside_wait is not None:
            beside_wait()
        receive(slot, nx)
        halo = got(slot, nx)
        s, l = iota(u.shape, 1), iota(u.shape, 2)
        r = r + jnp.where(s < w, c_ref[2] * spread_y(halo[2]), 0.0)
        r = r + jnp.where(s >= 8 - w, c_ref[3] * spread_y(halo[3]), 0.0)
        r = r + jnp.where(l < w, c_ref[4] * spread_z(halo[4], nx), 0.0)
        r = r + jnp.where(l >= 128 - w, c_ref[5] * spread_z(halo[5], nx), 0.0)
        low = r[0] + c_ref[0, 0] * halo[0]
        high = r[nx - 1] + c_ref[1, nx - 1] * halo[1]
        return jnp.concatenate([low[None], r[1:-1], high[None]], axis=0)

    def sweep(c_ref, u, b, w):
        return u + c_ref[7] * residual(c_ref, u, b, w)

    def coarse_residual(v, b):
        beside = coarse_shifts(v, sx, sy, False)
        r = b - c2[6] * v
        for d in range(6):
            r = r + c2[d] * beside[d]
        return r

    def coarse_sweep(v, b):
        return v + c2[7] * coarse_residual(v, b)

    def coarse_set_up():
        k = gather_wait(0)
        beside = coarse_shifts(k, sx, sy, True)
        total = jnp.zeros_like(k)
        faces = []
        for d in range(6):
            c = 4.0 * (0.5 * (k + beside[d]))
            c2[d] = c
            faces.append(c)
            total = total + c
        c2[6] = total
        c2[7] = 0.8 / total
        s, l = iota(k.shape, 1), iota(k.shape, 2)
        outer = [s < 2, s >= 6, s % 2 == 0, s % 2 == 1, l % 32 == 0, l % 32 == 31]
        outward = [
            jnp.sum(jnp.where(m, c, 0.0), axis=1, keepdims=True) for m, c in zip(outer, faces)
        ]
        block = iota((1, lz), 1) // 32

        def owners(i, j, shift):
            row = jnp.full((1, lz), -1, jnp.int32)
            if not (0 <= i < sx and 0 <= j < sy):
                return row
            for z in range(sz):
                if 0 <= z + shift < sz:
                    row = jnp.where(block == z, owner_ref[i, j, z + shift], row)
            return row

        label = iota((GROUPS, lz), 0)
        system = jnp.zeros((GROUPS, GROUPS), F32)
        for i in range(sx):
            for j in range(sy):
                at = i * sy + j
                mine = owners(i, j, 0) == label
                member = jnp.where(mine, 1.0, 0.0)
                member_ref[at] = member
                out = [o[at] for o in outward]
                terms = jnp.where(mine, out[0] + out[1] + out[2] + out[3] + out[4] + out[5], 0.0)
                near = [(i - 1, j, 0), (i + 1, j, 0), (i, j - 1, 0), (i, j + 1, 0),
                        (i, j, -1), (i, j, 1)]
                for d in range(6):
                    terms = terms - jnp.where(owners(*near[d]) == label, out[d], 0.0)
                system = system + lax.dot_general(
                    member, terms, (((1,), (1,)), ((), ())), precision=HIGHEST,
                    preferred_element_type=F32)
        rows, columns = iota((GROUPS, GROUPS), 0), iota((GROUPS, GROUPS), 1)

        def eliminate(step, a):
            at_row, at_column = rows == step, columns == step
            row = jnp.sum(jnp.where(at_row, a, 0.0), axis=0, keepdims=True)
            column = jnp.sum(jnp.where(at_column, a, 0.0), axis=1, keepdims=True)
            pivot = jnp.sum(jnp.where(at_column, row, 0.0), axis=1, keepdims=True)
            over = 1.0 / pivot[0:1]
            swept = a - column * (row * over)
            swept = jnp.where(at_row, row * over, swept)
            swept = jnp.where(at_column, column * over, swept)
            return jnp.where(at_row & at_column, -over, swept)

        return -lax.fori_loop(0, GROUPS, eliminate, system)

    diagonal = iota((GROUPS, GROUPS), 0) == iota((GROUPS, GROUPS), 1)

    def coarse_solve(b, inverse):
        v = c2[7] * b
        for _ in range(SWEEPS - 1):
            v = coarse_sweep(v, b)
        sums = jnp.sum(coarse_residual(v, b), axis=1, keepdims=True)
        grouped = jnp.zeros((GROUPS, lz), F32)
        for i in range(n_xy):
            grouped = grouped + member_ref[i] * sums[i]
        rc = jnp.sum(grouped, axis=1, keepdims=True)
        xc = jnp.sum(inverse * rc, axis=0, keepdims=True)
        xc = jnp.sum(jnp.where(diagonal, xc, 0.0), axis=1, keepdims=True)
        lifted = jnp.stack([
            jnp.sum(member_ref[i] * xc, axis=0, keepdims=True) for i in range(n_xy)
        ])
        v = v + lifted
        for _ in range(SWEEPS):
            v = coarse_sweep(v, b)
        for first in range(lz // 128):
            wide_ref[:, first] = v[:, :, first * 128 : first * 128 + 128]
        mine = wide_ref[my_xy, me[2] // 4]
        put = (iota((128, 128), 0) == lane_base + iota((128, 128), 1) // 4).astype(F32)
        mine = jnp.dot(mine, put, precision=HIGHEST, preferred_element_type=F32)
        low = iota((8, 128), 0) < 4
        return jnp.stack([
            jnp.where(low, mine[2 * x : 2 * x + 1], mine[2 * x + 1 : 2 * x + 2])
            for x in range(4)
        ])

    source = source_ref[...]
    inverse = None
    u = None
    for cycle in range(CYCLES):
        if cycle == 0:
            u = c0[7] * source
        else:
            u = sweep(c0, u, source, 1)
        for _ in range(SWEEPS - 1):
            u = sweep(c0, u, source, 1)
        b1 = restrict(residual(c0, u, source, 1), 1)
        u1 = c1[7] * b1
        for _ in range(SWEEPS - 1):
            u1 = sweep(c1, u1, b1, 2)
        b2 = restrict(residual(c1, u1, b1, 2), 2)
        gather_start(1 + cycle, b2)
        if cycle == 0:
            inverse = coarse_set_up()
        u1 = u1 + prolong(coarse_solve(gather_wait(1 + cycle), inverse))
        for _ in range(SWEEPS):
            u1 = sweep(c1, u1, b1, 2)
        u = u + prolong(u1)
        for _ in range(SWEEPS):
            u = sweep(c0, u, source, 1)
    sol_ref[...] = u
    res_ref[...] = residual(c0, u, source, 1)


def solution(mesh):
    sizes = tuple(mesh.shape[a] for a in AXES)
    sx, sy, sz = sizes
    count, n_xy, lz = sx * sy * sz, sx * sy, 32 * sz

    def on_device(source, conductivity, block_owner):
        vmem = pl.BlockSpec(memory_space=pltpu.VMEM)
        return pl.pallas_call(
            functools.partial(kernel, sizes),
            out_shape=[jax.ShapeDtypeStruct(source.shape, F32)] * 2,
            in_specs=[vmem, vmem, pl.BlockSpec(memory_space=pltpu.SMEM)],
            out_specs=[vmem, vmem],
            scratch_shapes=[
                pltpu.VMEM((4, 6, 16, 128), F32),
                pltpu.VMEM((4, 6, 16, 128), F32),
                pltpu.VMEM((3, 8, 128), F32),
                pltpu.VMEM((3, count, 8, 128), F32),
                pltpu.VMEM((8, 16, 8, 128), F32),
                pltpu.VMEM((8, 8, 8, 128), F32),
                pltpu.VMEM((8, n_xy, 8, lz), F32),
                pltpu.VMEM((n_xy, GROUPS, lz), F32),
                pltpu.VMEM((n_xy, lz // 128, 8, 128), F32),
                pltpu.SemaphoreType.DMA((4, 6)),
                pltpu.SemaphoreType.DMA((4, 6)),
                pltpu.SemaphoreType.DMA((3,)),
                pltpu.SemaphoreType.DMA((3,)),
            ],
            compiler_params=pltpu.CompilerParams(
                collective_id=0, has_side_effects=True, vmem_limit_bytes=48 * 1024 * 1024
            ),
        )(source, conductivity, block_owner)

    spec = P(*AXES)
    return jax.shard_map(
        on_device, mesh=mesh, in_specs=(spec, spec, P()), out_specs=(spec, spec), check_vma=False
    )
```

time: 676 us -> 79.6 us (0.12); the launches traced: 666 us -> 79.3 us
  starting transfers between devices: 406 us -> 0 us
  waiting for transfers between devices: 134 us -> 0 us
  Pallas kernels: 0 us -> 75 us
  blocking collectives: 58.4 us -> 0 us
  local copies, waits for them, and re-layouts: 39.1 us -> 3.62 us
  other arithmetic: 22.6 us -> 0 us
    ppermute x152 -> x0, starting transfers between devices: 406 us -> none  [the longest x76 308 us: padded_2(): before = lax.ppermute(last, axis, up)]
    ppermute x152 -> x0, waiting for transfers between devices: 134 us -> none  [the longest x76 68.9 us: padded_2(): before = lax.ppermute(last, axis, up)]
    pallas_call x0 -> x1, Pallas kernels: none -> 75 us  [on_device(): pl.pallas_call(functools.partial(kernel, sizes), out_shape=[jax.ShapeDtyp...]
    all_gather x3 -> x0, blocking collectives: 37.3 us -> none  [the longest x2 27.1 us: on_device(): lax.all_gather(next_rhs[None], ('gx', 'gy'), axis=0, tiled=True)]
    reshape x9 -> x0, local copies, waits for them, and re-layouts: 27.1 us -> none  [the longest x5 18.5 us: coarsen(): values.reshape(extent_x // 2, 2, extent_y // 2, 2, extent_z // 2, 2)]
    psum x2 -> x0, blocking collectives: 21.1 us -> none  [the longest x1 10.7 us: on_device(): factor = jnp.linalg.cholesky(lax.psum(system - coupled - coupled.T, 'gz'))]
    reduce_sum x16 -> x0, other arithmetic: 9.05 us -> none  [the longest x6 8.02 us: coarsen(): values.reshape(extent_x // 2, 2, extent_y // 2, 2, extent_z // 2, 2)]
  transfers between devices with their start and end apart: 152 -> 0, of which waited for: 89 -> 0; matrix products, arithmetic and copies ran while one was open for 4% -> 0% of each run, Pallas kernels for 0% -> 0%
where the time goes in v1:
time: 79.6 us; the launch traced here: 79.3 us
  Pallas kernels  75 us (94%)
  local copies, waits for them, and re-layouts  3.62 us (5%)
    pallas_call x1, Pallas kernels, on_device(): pl.pallas_call(functools.partial(kernel, sizes), out_shape=[jax.ShapeDtyp...  75 us
    unnamed x8, local copies, waits for them, and re-layouts  3.62 us

profile of v1, /device:TPU:0, one launch (start us, length us, event | category | flops | bytes accessed | tf_op | source)
XLA Modules:
  0.0 79.3 jit_solution(14779145115754597364)
XLA Ops:
  0.6 0.0 copy-start
  0.6 0.8 %copy-done = f32[16,8,128]{2,1,0:T(8,128)S(1)} copy-done((f32[16,8,128]{2,1,0:T(8,128)S(1)}, f32[16,8,128]{2,1,0:T(8,128)}, u32[]{:S(2)}) %copy-start) | copy-done | bytes 65560
  1.5 0.0 copy-start.1
  1.5 0.8 %copy-done.1 = f32[16,8,128]{2,1,0:T(8,128)S(1)} copy-done((f32[16,8,128]{2,1,0:T(8,128)S(1)}, f32[16,8,128]{2,1,0:T(8,128)}, u32[]{:S(2)}) %copy-start.1) | copy-done | bytes 65560
  2.3 0.0 copy-start.2
  2.3 0.7 copy-done.2
  3.0 75.0 %shard_map.50 = (f32[16,8,128]{2,1,0:T(8,128)S(1)}, f32[16,8,128]{2,1,0:T(8,128)S(1)}) custom-call(f32[16,8,128]{2,1,0:T(8,128)S(1)} %copy-done, f32[16,8,128]{2,1,0:T(8,128)S(1)} %copy-done.1, s32[2,4,4]{2,1,0:T(4,128)S(1)} %copy-done.2), custom_call_target="tpu_custom_call" | custom-call | tf_op jit(solution)/shard_map/pallas_call | solution.py:409
  78.0 0.6 copy.7
  78.6 0.6 copy.8
Async XLA Ops:
  0.6 0.8 %copy-start = (f32[16,8,128]{2,1,0:T(8,128)S(1)}, f32[16,8,128]{2,1,0:T(8,128)}, u32[]{:S(2)}) copy-start(f32[16,8,128]{2,1,0:T(8,128)} %source_ref.1) | copy-start | bytes 196612
  1.5 0.8 %copy-start.1 = (f32[16,8,128]{2,1,0:T(8,128)S(1)}, f32[16,8,128]{2,1,0:T(8,128)}, u32[]{:S(2)}) copy-start(f32[16,8,128]{2,1,0:T(8,128)} %k_ref.1) | copy-start | bytes 196612
  2.3 0.7 copy-start.2

commit v2 on v1

--- a/solution.py
+++ b/solution.py
@@ -101,28 +101,41 @@
 
 
 def kernel(sizes, source_ref, k_ref, owner_ref, sol_ref, res_ref,
-           sbuf, rbuf, gsend, gbuf, c0, c1, c2, member_ref, wide_ref,
-           ssem, rsem, gssem, grsem):
+           sbuf, rbuf, zbuf, gbuf, c0, c1, c2, member_ref, wide_ref, matrix_ref,
+           ssem, rsem, zssem, zrsem, gssem, grsem):
     sx, sy, sz = sizes
-    count, n_xy, lz = sx * sy * sz, sx * sy, 32 * sz
+    n_xy, lz = sx * sy, 32 * sz
     me = [lax.axis_index(a) for a in AXES]
     my_xy = me[0] * sy + me[1]
-    linear = my_xy * sz + me[2]
     edge = [me[0] == 0, me[0] == sx - 1, me[1] == 0, me[1] == sy - 1, me[2] == 0, me[2] == sz - 1]
 
     rbuf[...] = jnp.zeros_like(rbuf)
 
-    def coords(d):
-        t = lax.rem(linear + d, count)
-        return (t // (sy * sz), (t // sz) % sy, t % sz)
+    def line_peer(d):
+        t = me[2] + d
+        return (me[0], me[1], jnp.where(t >= sz, t - sz, t))
+
+    def plane_peer(d):
+        t = my_xy + d
+        t = jnp.where(t >= n_xy, t - n_xy, t)
+        return (t // sy, t % sy, me[2])
+
+    def over_plane(body):
+        if n_xy <= 8:
+            for d in range(1, n_xy):
+                body(d)
+        else:
+            pl.loop(1, n_xy)(body)
 
     barrier = pltpu.get_barrier_semaphore()
 
-    @pl.loop(1, count)
-    def _(d):
-        pl.semaphore_signal(barrier, inc=1, device_id=coords(d), device_id_type=MESH)
-
-    pl.semaphore_wait(barrier, count - 1)
+    def greet(there):
+        pl.semaphore_signal(barrier, inc=1, device_id=there, device_id_type=MESH)
+
+    for d in range(1, sz):
+        greet(line_peer(d))
+    over_plane(lambda d: greet(plane_peer(d)))
+    pl.semaphore_wait(barrier, sz - 1 + n_xy - 1)
 
     def copy_of(slot, d, nx):
         axis, step = d // 2, 1 if d % 2 else -1
@@ -145,6 +158,7 @@
             else:
                 sbuf[slot, d, 0:8, :] = faces[d]
 
+        for d in (4, 5, 2, 3, 0, 1):
             @pl.when(jnp.logical_not(edge[d]))
             def _():
                 copy_of(slot, d, nx).start()
@@ -170,15 +184,29 @@
 
     lane_base = (me[2] % 4) * 32
 
-    def gather_copy(use, d):
+    def line_copy(use, d):
         return pltpu.make_async_remote_copy(
-            src_ref=gsend.at[use],
-            dst_ref=gbuf.at[use, linear],
+            src_ref=zbuf.at[use, me[2]],
+            dst_ref=zbuf.at[use, me[2]],
+            send_sem=zssem.at[use],
+            recv_sem=zrsem.at[use],
+            device_id=line_peer(d),
+            device_id_type=MESH,
+        )
+
+    def plane_copy(use, d):
+        return pltpu.make_async_remote_copy(
+            src_ref=gbuf.at[use, my_xy],
+            dst_ref=gbuf.at[use, my_xy],
             send_sem=gssem.at[use],
             recv_sem=grsem.at[use],
-            device_id=coords(d),
+            device_id=plane_peer(d),
             device_id_type=MESH,
         )
+
+    def await_all(ref, send_sem, recv_sem):
+        pltpu.make_async_copy(ref, ref, send_sem).wait()
+        pltpu.make_async_copy(ref, ref, recv_sem).wait()
 
     def gather_start(use, v):
         s = iota((8, 128), 0)
@@ -189,25 +217,24 @@
             packed = jnp.where(s // 2 == x, both, packed)
         pick = (iota((128, 128), 0) == 4 * (iota((128, 128), 1) - lane_base)).astype(F32)
         packed = jnp.dot(packed, pick, precision=HIGHEST, preferred_element_type=F32)
-        gsend[use] = packed
-        gbuf[use, linear] = packed
-
-        @pl.loop(1, count)
-        def _(d):
-            gather_copy(use, d).start()
+        zbuf[use, me[2]] = packed
+        for d in range(1, sz):
+            line_copy(use, d).start()
+
+    def gather_next(use):
+        await_all(zbuf.at[use, pl.ds(0, sz - 1)], zssem.at[use], zrsem.at[use])
+        for group in range(lz // 128):
+            part = zbuf[use, 4 * group]
+            for j in range(4 * group + 1, 4 * group + 4):
+                part = part + zbuf[use, j]
+            gbuf[use, my_xy, group] = part
+        over_plane(lambda d: plane_copy(use, d).start())
 
     def gather_wait(use):
-        whole = gbuf.at[use, pl.ds(0, count - 1)]
-        pltpu.make_async_copy(whole, whole, gssem.at[use]).wait()
-        pltpu.make_async_copy(whole, whole, grsem.at[use]).wait()
+        await_all(gbuf.at[use, pl.ds(0, n_xy - 1)], gssem.at[use], grsem.at[use])
         rows = []
         for i in range(n_xy):
-            parts = []
-            for first in range(0, sz, 4):
-                part = gbuf[use, i * sz + first]
-                for j in range(first + 1, min(first + 4, sz)):
-                    part = part + gbuf[use, i * sz + j]
-                parts.append(part)
+            parts = [gbuf[use, i, group] for group in range(lz // 128)]
             rows.append(parts[0] if len(parts) == 1 else jnp.concatenate(parts, axis=1))
         return jnp.stack(rows)
 
@@ -242,6 +269,7 @@
     receive(0, 16)
     set_up(c0, k0, k0_faces, got(0, 16), 1)
     receive(1, 8)
+    gather_next(0)
     set_up(c1, k1, k1_faces, got(1, 8), 2)
 
     phase = [0]
@@ -268,8 +296,8 @@
         high = r[nx - 1] + c_ref[1, nx - 1] * halo[1]
         return jnp.concatenate([low[None], r[1:-1], high[None]], axis=0)
 
-    def sweep(c_ref, u, b, w):
-        return u + c_ref[7] * residual(c_ref, u, b, w)
+    def sweep(c_ref, u, b, w, beside_wait=None):
+        return u + c_ref[7] * residual(c_ref, u, b, w, beside_wait)
 
     def coarse_residual(v, b):
         beside = coarse_shifts(v, sx, sy, False)
@@ -326,20 +354,19 @@
                 system = system + lax.dot_general(
                     member, terms, (((1,), (1,)), ((), ())), precision=HIGHEST,
                     preferred_element_type=F32)
+        matrix_ref[...] = system
+
+    def eliminate(first, last):
         rows, columns = iota((GROUPS, GROUPS), 0), iota((GROUPS, GROUPS), 1)
-
-        def eliminate(step, a):
+        a = matrix_ref[...]
+        for step in range(first, last):
             at_row, at_column = rows == step, columns == step
-            row = jnp.sum(jnp.where(at_row, a, 0.0), axis=0, keepdims=True)
-            column = jnp.sum(jnp.where(at_column, a, 0.0), axis=1, keepdims=True)
-            pivot = jnp.sum(jnp.where(at_column, row, 0.0), axis=1, keepdims=True)
-            over = 1.0 / pivot[0:1]
-            swept = a - column * (row * over)
-            swept = jnp.where(at_row, row * over, swept)
-            swept = jnp.where(at_column, column * over, swept)
-            return jnp.where(at_row & at_column, -over, swept)
-
-        return -lax.fori_loop(0, GROUPS, eliminate, system)
+            over = 1.0 / jnp.broadcast_to(a[step : step + 1, step : step + 1], (1, GROUPS))
+            row = a[step : step + 1, :] * over
+            column = jnp.broadcast_to(a[:, step : step + 1], (GROUPS, GROUPS))
+            swept = jnp.where(at_column, column * over, a - column * row)
+            a = jnp.where(at_row, jnp.where(at_column, -over, row), swept)
+        matrix_ref[...] = a
 
     diagonal = iota((GROUPS, GROUPS), 0) == iota((GROUPS, GROUPS), 1)
 
@@ -371,25 +398,26 @@
             for x in range(4)
         ])
 
+    def part(first, last):
+        return lambda: eliminate(first, last)
+
     source = source_ref[...]
-    inverse = None
     u = None
     for cycle in range(CYCLES):
-        if cycle == 0:
-            u = c0[7] * source
-        else:
-            u = sweep(c0, u, source, 1)
-        for _ in range(SWEEPS - 1):
-            u = sweep(c0, u, source, 1)
-        b1 = restrict(residual(c0, u, source, 1), 1)
+        first = cycle == 0
+        u = c0[7] * source if first else sweep(c0, u, source, 1)
+        u = sweep(c0, u, source, 1, coarse_set_up if first else None)
+        b1 = restrict(residual(c0, u, source, 1, part(0, 4) if first else None), 1)
         u1 = c1[7] * b1
-        for _ in range(SWEEPS - 1):
-            u1 = sweep(c1, u1, b1, 2)
-        b2 = restrict(residual(c1, u1, b1, 2), 2)
+        u1 = sweep(c1, u1, b1, 2, part(4, 8) if first else None)
+        b2 = restrict(residual(c1, u1, b1, 2, part(8, 12) if first else None), 2)
         gather_start(1 + cycle, b2)
-        if cycle == 0:
-            inverse = coarse_set_up()
-        u1 = u1 + prolong(coarse_solve(gather_wait(1 + cycle), inverse))
+        if first:
+            eliminate(12, 14)
+        gather_next(1 + cycle)
+        if first:
+            eliminate(14, 16)
+        u1 = u1 + prolong(coarse_solve(gather_wait(1 + cycle), -matrix_ref[...]))
         for _ in range(SWEEPS):
             u1 = sweep(c1, u1, b1, 2)
         u = u + prolong(u1)
@@ -402,7 +430,7 @@
 def solution(mesh):
     sizes = tuple(mesh.shape[a] for a in AXES)
     sx, sy, sz = sizes
-    count, n_xy, lz = sx * sy * sz, sx * sy, 32 * sz
+    n_xy, lz = sx * sy, 32 * sz
 
     def on_device(source, conductivity, block_owner):
         vmem = pl.BlockSpec(memory_space=pltpu.VMEM)
@@ -414,15 +442,18 @@
             scratch_shapes=[
                 pltpu.VMEM((4, 6, 16, 128), F32),
                 pltpu.VMEM((4, 6, 16, 128), F32),
-                pltpu.VMEM((3, 8, 128), F32),
-                pltpu.VMEM((3, count, 8, 128), F32),
+                pltpu.VMEM((3, sz, 8, 128), F32),
+                pltpu.VMEM((3, n_xy, lz // 128, 8, 128), F32),
                 pltpu.VMEM((8, 16, 8, 128), F32),
                 pltpu.VMEM((8, 8, 8, 128), F32),
                 pltpu.VMEM((8, n_xy, 8, lz), F32),
                 pltpu.VMEM((n_xy, GROUPS, lz), F32),
                 pltpu.VMEM((n_xy, lz // 128, 8, 128), F32),
+                pltpu.VMEM((GROUPS, GROUPS), F32),
                 pltpu.SemaphoreType.DMA((4, 6)),
                 pltpu.SemaphoreType.DMA((4, 6)),
+                pltpu.SemaphoreType.DMA((3,)),
+                pltpu.SemaphoreType.DMA((3,)),
                 pltpu.SemaphoreType.DMA((3,)),
                 pltpu.SemaphoreType.DMA((3,)),
             ],

time: 79.6 us -> 82.6 us (1.038)
  Pallas kernels: 75 us -> 78.1 us
    pallas_call x1, Pallas kernels: 75 us -> 78.1 us  [on_device(): pl.pallas_call(functools.partial(kernel, sizes), out_shape=[jax.ShapeDtyp...]
where the time goes in v2:
time: 82.6 us; the launch traced here: 82.4 us
  Pallas kernels  78.1 us (95%)
  local copies, waits for them, and re-layouts  3.62 us (4%)
    pallas_call x1, Pallas kernels, on_device(): pl.pallas_call(functools.partial(kernel, sizes), out_shape=[jax.ShapeDtyp...  78.1 us
    unnamed x8, local copies, waits for them, and re-layouts  3.62 us

profile of v2, /device:TPU:0, one launch (start us, length us, event | category | flops | bytes accessed | tf_op | source)
XLA Modules:
  0.0 82.4 jit_solution(3593253415496875851)
XLA Ops:
  0.6 0.0 copy-start
  0.6 0.8 %copy-done = f32[16,8,128]{2,1,0:T(8,128)S(1)} copy-done((f32[16,8,128]{2,1,0:T(8,128)S(1)}, f32[16,8,128]{2,1,0:T(8,128)}, u32[]{:S(2)}) %copy-start) | copy-done | bytes 65560
  1.5 0.0 copy-start.1
  1.5 0.8 %copy-done.1 = f32[16,8,128]{2,1,0:T(8,128)S(1)} copy-done((f32[16,8,128]{2,1,0:T(8,128)S(1)}, f32[16,8,128]{2,1,0:T(8,128)}, u32[]{:S(2)}) %copy-start.1) | copy-done | bytes 65560
  2.3 0.0 copy-start.2
  2.3 0.7 copy-done.2
  3.0 78.1 %shard_map.50 = (f32[16,8,128]{2,1,0:T(8,128)S(1)}, f32[16,8,128]{2,1,0:T(8,128)S(1)}) custom-call(f32[16,8,128]{2,1,0:T(8,128)S(1)} %copy-done, f32[16,8,128]{2,1,0:T(8,128)S(1)} %copy-done.1, s32[2,4,4]{2,1,0:T(4,128)S(1)} %copy-done.2), custom_call_target="tpu_custom_call" | custom-call | tf_op jit(solution)/shard_map/pallas_call | solution.py:437
  81.1 0.6 copy.7
  81.7 0.6 copy.8
Async XLA Ops:
  0.6 0.8 %copy-start = (f32[16,8,128]{2,1,0:T(8,128)S(1)}, f32[16,8,128]{2,1,0:T(8,128)}, u32[]{:S(2)}) copy-start(f32[16,8,128]{2,1,0:T(8,128)} %source_ref.1) | copy-start | bytes 196612
  1.5 0.8 %copy-start.1 = (f32[16,8,128]{2,1,0:T(8,128)S(1)}, f32[16,8,128]{2,1,0:T(8,128)}, u32[]{:S(2)}) copy-start(f32[16,8,128]{2,1,0:T(8,128)} %k_ref.1) | copy-start | bytes 196612
  2.3 0.7 copy-start.2

commit v3 on v1

--- a/solution.py
+++ b/solution.py
@@ -101,7 +101,7 @@
 
 
 def kernel(sizes, source_ref, k_ref, owner_ref, sol_ref, res_ref,
-           sbuf, rbuf, gsend, gbuf, c0, c1, c2, member_ref, wide_ref,
+           sbuf, rbuf, gsend, gbuf, c0, c1, c2, member_ref, wide_ref, matrix_ref,
            ssem, rsem, gssem, grsem):
     sx, sy, sz = sizes
     count, n_xy, lz = sx * sy * sz, sx * sy, 32 * sz
@@ -268,8 +268,8 @@
         high = r[nx - 1] + c_ref[1, nx - 1] * halo[1]
         return jnp.concatenate([low[None], r[1:-1], high[None]], axis=0)
 
-    def sweep(c_ref, u, b, w):
-        return u + c_ref[7] * residual(c_ref, u, b, w)
+    def sweep(c_ref, u, b, w, beside_wait=None):
+        return u + c_ref[7] * residual(c_ref, u, b, w, beside_wait)
 
     def coarse_residual(v, b):
         beside = coarse_shifts(v, sx, sy, False)
@@ -326,20 +326,19 @@
                 system = system + lax.dot_general(
                     member, terms, (((1,), (1,)), ((), ())), precision=HIGHEST,
                     preferred_element_type=F32)
+        matrix_ref[...] = system
+
+    def eliminate(first, last):
         rows, columns = iota((GROUPS, GROUPS), 0), iota((GROUPS, GROUPS), 1)
-
-        def eliminate(step, a):
+        a = matrix_ref[...]
+        for step in range(first, last):
             at_row, at_column = rows == step, columns == step
-            row = jnp.sum(jnp.where(at_row, a, 0.0), axis=0, keepdims=True)
-            column = jnp.sum(jnp.where(at_column, a, 0.0), axis=1, keepdims=True)
-            pivot = jnp.sum(jnp.where(at_column, row, 0.0), axis=1, keepdims=True)
-            over = 1.0 / pivot[0:1]
-            swept = a - column * (row * over)
-            swept = jnp.where(at_row, row * over, swept)
-            swept = jnp.where(at_column, column * over, swept)
-            return jnp.where(at_row & at_column, -over, swept)
-
-        return -lax.fori_loop(0, GROUPS, eliminate, system)
+            over = 1.0 / jnp.broadcast_to(a[step : step + 1, step : step + 1], (1, GROUPS))
+            row = a[step : step + 1, :] * over
+            column = jnp.broadcast_to(a[:, step : step + 1], (GROUPS, GROUPS))
+            swept = jnp.where(at_column, column * over, a - column * row)
+            a = jnp.where(at_row, jnp.where(at_column, -over, row), swept)
+        matrix_ref[...] = a
 
     diagonal = iota((GROUPS, GROUPS), 0) == iota((GROUPS, GROUPS), 1)
 
@@ -371,25 +370,23 @@
             for x in range(4)
         ])
 
+    def part(first, last):
+        return lambda: eliminate(first, last)
+
     source = source_ref[...]
-    inverse = None
     u = None
     for cycle in range(CYCLES):
-        if cycle == 0:
-            u = c0[7] * source
-        else:
-            u = sweep(c0, u, source, 1)
-        for _ in range(SWEEPS - 1):
-            u = sweep(c0, u, source, 1)
-        b1 = restrict(residual(c0, u, source, 1), 1)
+        first = cycle == 0
+        u = c0[7] * source if first else sweep(c0, u, source, 1)
+        u = sweep(c0, u, source, 1, coarse_set_up if first else None)
+        b1 = restrict(residual(c0, u, source, 1, part(0, 4) if first else None), 1)
         u1 = c1[7] * b1
-        for _ in range(SWEEPS - 1):
-            u1 = sweep(c1, u1, b1, 2)
-        b2 = restrict(residual(c1, u1, b1, 2), 2)
+        u1 = sweep(c1, u1, b1, 2, part(4, 8) if first else None)
+        b2 = restrict(residual(c1, u1, b1, 2, part(8, 12) if first else None), 2)
         gather_start(1 + cycle, b2)
-        if cycle == 0:
-            inverse = coarse_set_up()
-        u1 = u1 + prolong(coarse_solve(gather_wait(1 + cycle), inverse))
+        if first:
+            eliminate(12, 16)
+        u1 = u1 + prolong(coarse_solve(gather_wait(1 + cycle), -matrix_ref[...]))
         for _ in range(SWEEPS):
             u1 = sweep(c1, u1, b1, 2)
         u = u + prolong(u1)
@@ -421,6 +418,7 @@
                 pltpu.VMEM((8, n_xy, 8, lz), F32),
                 pltpu.VMEM((n_xy, GROUPS, lz), F32),
                 pltpu.VMEM((n_xy, lz // 128, 8, 128), F32),
+                pltpu.VMEM((GROUPS, GROUPS), F32),
                 pltpu.SemaphoreType.DMA((4, 6)),
                 pltpu.SemaphoreType.DMA((4, 6)),
                 pltpu.SemaphoreType.DMA((3,)),

time: 79.6 us -> 80.2 us (level)
  no operation moved by 1% of the time
where the time goes in v3:
time: 80.2 us; the launch traced here: 79.9 us
  Pallas kernels  75.6 us (94%)
  local copies, waits for them, and re-layouts  3.62 us (5%)
    pallas_call x1, Pallas kernels, on_device(): pl.pallas_call(functools.partial(kernel, sizes), out_shape=[jax.ShapeDtyp...  75.6 us
    unnamed x8, local copies, waits for them, and re-layouts  3.62 us

profile of v3, /device:TPU:0, one launch (start us, length us, event | category | flops | bytes accessed | tf_op | source)
XLA Modules:
  0.0 79.9 jit_solution(10497069200989252865)
XLA Ops:
  0.6 0.0 copy-start
  0.6 0.8 %copy-done = f32[16,8,128]{2,1,0:T(8,128)S(1)} copy-done((f32[16,8,128]{2,1,0:T(8,128)S(1)}, f32[16,8,128]{2,1,0:T(8,128)}, u32[]{:S(2)}) %copy-start) | copy-done | bytes 65560
  1.5 0.0 copy-start.1
  1.5 0.8 %copy-done.1 = f32[16,8,128]{2,1,0:T(8,128)S(1)} copy-done((f32[16,8,128]{2,1,0:T(8,128)S(1)}, f32[16,8,128]{2,1,0:T(8,128)}, u32[]{:S(2)}) %copy-start.1) | copy-done | bytes 65560
  2.3 0.0 copy-start.2
  2.3 0.7 copy-done.2
  3.0 75.6 %shard_map.50 = (f32[16,8,128]{2,1,0:T(8,128)S(1)}, f32[16,8,128]{2,1,0:T(8,128)S(1)}) custom-call(f32[16,8,128]{2,1,0:T(8,128)S(1)} %copy-done, f32[16,8,128]{2,1,0:T(8,128)S(1)} %copy-done.1, s32[2,4,4]{2,1,0:T(4,128)S(1)} %copy-done.2), custom_call_target="tpu_custom_call" | custom-call | tf_op jit(solution)/shard_map/pallas_call | solution.py:406
  78.6 0.6 copy.7
  79.3 0.6 copy.8
Async XLA Ops:
  0.6 0.8 %copy-start = (f32[16,8,128]{2,1,0:T(8,128)S(1)}, f32[16,8,128]{2,1,0:T(8,128)}, u32[]{:S(2)}) copy-start(f32[16,8,128]{2,1,0:T(8,128)} %source_ref.1) | copy-start | bytes 196612
  1.5 0.8 %copy-start.1 = (f32[16,8,128]{2,1,0:T(8,128)S(1)}, f32[16,8,128]{2,1,0:T(8,128)}, u32[]{:S(2)}) copy-start(f32[16,8,128]{2,1,0:T(8,128)} %k_ref.1) | copy-start | bytes 196612
  2.3 0.7 copy-start.2

commit v4 on v1

--- a/solution.py
+++ b/solution.py
@@ -116,12 +116,29 @@
         t = lax.rem(linear + d, count)
         return (t // (sy * sz), (t // sz) % sy, t % sz)
 
+    def wrapped(a, step, size):
+        t = me[a] + step
+        return jnp.where(t >= size, t - size, t) if step else t
+
+    def to_others(body):
+        if count <= 64:
+            tx = [wrapped(0, d, sx) for d in range(sx)]
+            ty = [wrapped(1, d, sy) for d in range(sy)]
+            tz = [wrapped(2, d, sz) for d in range(sz)]
+            for i in range(sx):
+                for j in range(sy):
+                    for k in range(sz):
+                        if i or j or k:
+                            body((tx[i], ty[j], tz[k]))
+        else:
+            pl.loop(1, count)(lambda d: body(coords(d)))
+
     barrier = pltpu.get_barrier_semaphore()
 
-    @pl.loop(1, count)
-    def _(d):
-        pl.semaphore_signal(barrier, inc=1, device_id=coords(d), device_id_type=MESH)
-
+    def greet(there):
+        pl.semaphore_signal(barrier, inc=1, device_id=there, device_id_type=MESH)
+
+    to_others(greet)
     pl.semaphore_wait(barrier, count - 1)
 
     def copy_of(slot, d, nx):
@@ -138,7 +155,7 @@
         )
 
     def send(slot, faces, nx):
-        for d in (4, 5, 2, 3, 0, 1):
+        for d in (0, 1, 2, 3, 4, 5):
             if d in (2, 3):
                 for x in range(nx):
                     sbuf[slot, d, x : x + 1, :] = faces[d][x]
@@ -149,12 +166,16 @@
             def _():
                 copy_of(slot, d, nx).start()
 
+    pending = []
+
     def receive(slot, nx):
+        before = pending.pop() if pending else None
+        pending.append((slot, nx))
         for d in range(6):
             @pl.when(jnp.logical_not(edge[d]))
             def _():
-                copy = copy_of(slot, d, nx)
-                copy.wait_send()
+                if before:
+                    copy_of(before[0], d, before[1]).wait_send()
                 rows = nx if d // 2 == 1 else 8
                 pltpu.make_async_copy(
                     rbuf.at[slot, d, pl.ds(0, rows)], rbuf.at[slot, d, pl.ds(0, rows)],
@@ -170,13 +191,13 @@
 
     lane_base = (me[2] % 4) * 32
 
-    def gather_copy(use, d):
+    def gather_copy(use, there):
         return pltpu.make_async_remote_copy(
             src_ref=gsend.at[use],
             dst_ref=gbuf.at[use, linear],
             send_sem=gssem.at[use],
             recv_sem=grsem.at[use],
-            device_id=coords(d),
+            device_id=there,
             device_id_type=MESH,
         )
 
@@ -187,26 +208,30 @@
         for x in range(4):
             both = jnp.where(straight, v[x], pltpu.roll(v[x], 4, 0))
             packed = jnp.where(s // 2 == x, both, packed)
-        pick = (iota((128, 128), 0) == 4 * (iota((128, 128), 1) - lane_base)).astype(F32)
+        pick = (iota((128, 128), 0) == 4 * (iota((128, 128), 1) % 32)).astype(F32)
         packed = jnp.dot(packed, pick, precision=HIGHEST, preferred_element_type=F32)
-        gsend[use] = packed
-        gbuf[use, linear] = packed
-
-        @pl.loop(1, count)
-        def _(d):
-            gather_copy(use, d).start()
+        part = iota((1, 128), 1) // 32
+        for y in range(2):
+            row = packed[y : y + 1]
+            for x in range(1, 4):
+                row = jnp.where(part == x, packed[2 * x + y : 2 * x + y + 1], row)
+            gsend[use, y : y + 1, :] = row
+            gbuf[use, linear, y : y + 1, :] = row
+        to_others(lambda there: gather_copy(use, there).start())
 
     def gather_wait(use):
         whole = gbuf.at[use, pl.ds(0, count - 1)]
-        pltpu.make_async_copy(whole, whole, gssem.at[use]).wait()
         pltpu.make_async_copy(whole, whole, grsem.at[use]).wait()
+        turn = (iota((8, 128), 1) // 32 - iota((8, 128), 0) // 2 + 4) % 4
         rows = []
         for i in range(n_xy):
             parts = []
             for first in range(0, sz, 4):
-                part = gbuf[use, i * sz + first]
-                for j in range(first + 1, min(first + 4, sz)):
-                    part = part + gbuf[use, i * sz + j]
+                four = jnp.concatenate([gbuf[use, i * sz + first + j] for j in range(4)], axis=0)
+                part = four
+                for t in range(1, 4):
+                    part = jnp.where(
+                        turn == t, pltpu.roll(pltpu.roll(four, 32 * t, 1), 8 - 2 * t, 0), part)
                 parts.append(part)
             rows.append(parts[0] if len(parts) == 1 else jnp.concatenate(parts, axis=1))
         return jnp.stack(rows)
@@ -397,6 +422,14 @@
             u = sweep(c0, u, source, 1)
     sol_ref[...] = u
     res_ref[...] = residual(c0, u, source, 1)
+    for slot, nx in pending:
+        for d in range(6):
+            @pl.when(jnp.logical_not(edge[d]))
+            def _():
+                copy_of(slot, d, nx).wait_send()
+    for use in range(1 + CYCLES):
+        whole = gbuf.at[use, pl.ds(0, count - 1)]
+        pltpu.make_async_copy(whole, whole, gssem.at[use]).wait()
 
 
 def solution(mesh):
@@ -414,8 +447,8 @@
             scratch_shapes=[
                 pltpu.VMEM((4, 6, 16, 128), F32),
                 pltpu.VMEM((4, 6, 16, 128), F32),
-                pltpu.VMEM((3, 8, 128), F32),
-                pltpu.VMEM((3, count, 8, 128), F32),
+                pltpu.VMEM((3, 2, 128), F32),
+                pltpu.VMEM((3, count, 2, 128), F32),
                 pltpu.VMEM((8, 16, 8, 128), F32),
                 pltpu.VMEM((8, 8, 8, 128), F32),
                 pltpu.VMEM((8, n_xy, 8, lz), F32),

time: 79.6 us -> 77.3 us (0.971)
  Pallas kernels: 75 us -> 72.8 us
    pallas_call x1, Pallas kernels: 75 us -> 72.8 us  [on_device(): pl.pallas_call(functools.partial(kernel, sizes), out_shape=[jax.ShapeDtyp...]
where the time goes in v4:
time: 77.3 us; the launch traced here: 77 us
  Pallas kernels  72.8 us (94%)
  local copies, waits for them, and re-layouts  3.62 us (5%)
    pallas_call x1, Pallas kernels, on_device(): pl.pallas_call(functools.partial(kernel, sizes), out_shape=[jax.ShapeDtyp...  72.8 us
    unnamed x8, local copies, waits for them, and re-layouts  3.62 us

profile of v4, /device:TPU:0, one launch (start us, length us, event | category | flops | bytes accessed | tf_op | source)
XLA Modules:
  0.0 77.0 jit_solution(1828839504715838917)
XLA Ops:
  0.6 0.0 copy-start
  0.6 0.8 %copy-done = f32[16,8,128]{2,1,0:T(8,128)S(1)} copy-done((f32[16,8,128]{2,1,0:T(8,128)S(1)}, f32[16,8,128]{2,1,0:T(8,128)}, u32[]{:S(2)}) %copy-start) | copy-done | bytes 65560
  1.5 0.0 copy-start.1
  1.5 0.8 %copy-done.1 = f32[16,8,128]{2,1,0:T(8,128)S(1)} copy-done((f32[16,8,128]{2,1,0:T(8,128)S(1)}, f32[16,8,128]{2,1,0:T(8,128)}, u32[]{:S(2)}) %copy-start.1) | copy-done | bytes 65560
  2.3 0.0 copy-start.2
  2.3 0.7 copy-done.2
  3.0 72.8 %shard_map.50 = (f32[16,8,128]{2,1,0:T(8,128)S(1)}, f32[16,8,128]{2,1,0:T(8,128)S(1)}) custom-call(f32[16,8,128]{2,1,0:T(8,128)S(1)} %copy-done, f32[16,8,128]{2,1,0:T(8,128)S(1)} %copy-done.1, s32[2,4,4]{2,1,0:T(4,128)S(1)} %copy-done.2), custom_call_target="tpu_custom_call" | custom-call | tf_op jit(solution)/shard_map/pallas_call | solution.py:442
  75.8 0.6 copy.7
  76.4 0.6 copy.8
Async XLA Ops:
  0.6 0.8 %copy-start = (f32[16,8,128]{2,1,0:T(8,128)S(1)}, f32[16,8,128]{2,1,0:T(8,128)}, u32[]{:S(2)}) copy-start(f32[16,8,128]{2,1,0:T(8,128)} %source_ref.1) | copy-start | bytes 196612
  1.5 0.8 %copy-start.1 = (f32[16,8,128]{2,1,0:T(8,128)S(1)}, f32[16,8,128]{2,1,0:T(8,128)}, u32[]{:S(2)}) copy-start(f32[16,8,128]{2,1,0:T(8,128)} %k_ref.1) | copy-start | bytes 196612
  2.3 0.7 copy-start.2

commit v5 on v4

--- a/solution.py
+++ b/solution.py
@@ -271,30 +271,37 @@
 
     phase = [0]
 
-    def residual(c_ref, u, b, w, beside_wait=None):
+    def residual(c_ref, u, b, w, lift=None):
         nx = u.shape[0]
+        if lift is None:
+            phase[0] += 1
         slot = 2 + phase[0] % 2
-        phase[0] += 1
-        send(slot, own_faces(u), nx)
+        if lift is None:
+            send(slot, own_faces(u), nx)
         inner = rolled(u, w)
         r = b - c_ref[6] * u
         for d in range(6):
             r = r + c_ref[d] * inner[d]
-        if beside_wait is not None:
-            beside_wait()
-        receive(slot, nx)
+        if lift is None:
+            receive(slot, nx)
         halo = got(slot, nx)
         s, l = iota(u.shape, 1), iota(u.shape, 2)
         r = r + jnp.where(s < w, c_ref[2] * spread_y(halo[2]), 0.0)
         r = r + jnp.where(s >= 8 - w, c_ref[3] * spread_y(halo[3]), 0.0)
         r = r + jnp.where(l < w, c_ref[4] * spread_z(halo[4], nx), 0.0)
         r = r + jnp.where(l >= 128 - w, c_ref[5] * spread_z(halo[5], nx), 0.0)
+        if lift is not None:
+            inside = [s < w, s >= 8 - w, l < w, l >= 128 - w]
+            for d in range(2, 6):
+                r = r + jnp.where(inside[d - 2], c_ref[d] * lift[d], 0.0)
+            halo[0] = halo[0] + lift[0][0]
+            halo[1] = halo[1] + lift[1][nx - 1]
         low = r[0] + c_ref[0, 0] * halo[0]
         high = r[nx - 1] + c_ref[1, nx - 1] * halo[1]
         return jnp.concatenate([low[None], r[1:-1], high[None]], axis=0)
 
-    def sweep(c_ref, u, b, w):
-        return u + c_ref[7] * residual(c_ref, u, b, w)
+    def sweep(c_ref, u, b, w, lift=None):
+        return u + c_ref[7] * residual(c_ref, u, b, w, lift)
 
     def coarse_residual(v, b):
         beside = coarse_shifts(v, sx, sy, False)
@@ -385,16 +392,24 @@
         v = v + lifted
         for _ in range(SWEEPS):
             v = coarse_sweep(v, b)
-        for first in range(lz // 128):
-            wide_ref[:, first] = v[:, :, first * 128 : first * 128 + 128]
-        mine = wide_ref[my_xy, me[2] // 4]
+        fields = [v] + coarse_shifts(v, sx, sy, False)
+        for f in range(7):
+            for first in range(lz // 128):
+                wide_ref[f, :, first] = fields[f][:, :, first * 128 : first * 128 + 128]
+        mine = jnp.concatenate([wide_ref[f, my_xy, me[2] // 4] for f in range(7)], axis=0)
         put = (iota((128, 128), 0) == lane_base + iota((128, 128), 1) // 4).astype(F32)
         mine = jnp.dot(mine, put, precision=HIGHEST, preferred_element_type=F32)
         low = iota((8, 128), 0) < 4
-        return jnp.stack([
-            jnp.where(low, mine[2 * x : 2 * x + 1], mine[2 * x + 1 : 2 * x + 2])
-            for x in range(4)
-        ])
+
+        def on_level_one(f):
+            at = 8 * f
+            return prolong(jnp.stack([
+                jnp.where(low, mine[at + 2 * x : at + 2 * x + 1],
+                          mine[at + 2 * x + 1 : at + 2 * x + 2])
+                for x in range(4)
+            ]))
+
+        return on_level_one(0), [on_level_one(f) for f in range(1, 7)]
 
     source = source_ref[...]
     inverse = None
@@ -414,8 +429,9 @@
         gather_start(1 + cycle, b2)
         if cycle == 0:
             inverse = coarse_set_up()
-        u1 = u1 + prolong(coarse_solve(gather_wait(1 + cycle), inverse))
-        for _ in range(SWEEPS):
+        correction, lift = coarse_solve(gather_wait(1 + cycle), inverse)
+        u1 = sweep(c1, u1 + correction, b1, 2, lift)
+        for _ in range(SWEEPS - 1):
             u1 = sweep(c1, u1, b1, 2)
         u = u + prolong(u1)
         for _ in range(SWEEPS):
@@ -453,7 +469,7 @@
                 pltpu.VMEM((8, 8, 8, 128), F32),
                 pltpu.VMEM((8, n_xy, 8, lz), F32),
                 pltpu.VMEM((n_xy, GROUPS, lz), F32),
-                pltpu.VMEM((n_xy, lz // 128, 8, 128), F32),
+                pltpu.VMEM((7, n_xy, lz // 128, 8, 128), F32),
                 pltpu.SemaphoreType.DMA((4, 6)),
                 pltpu.SemaphoreType.DMA((4, 6)),
                 pltpu.SemaphoreType.DMA((3,)),

time: 77.3 us -> 72.1 us (0.933)
  Pallas kernels: 72.8 us -> 67.6 us
    pallas_call x1, Pallas kernels: 72.8 us -> 67.6 us  [on_device(): pl.pallas_call(functools.partial(kernel, sizes), out_shape=[jax.ShapeDtyp...]
where the time goes in v5:
time: 72.1 us; the launch traced here: 71.9 us
  Pallas kernels  67.6 us (94%)
  local copies, waits for them, and re-layouts  3.62 us (5%)
    pallas_call x1, Pallas kernels, on_device(): pl.pallas_call(functools.partial(kernel, sizes), out_shape=[jax.ShapeDtyp...  67.6 us
    unnamed x8, local copies, waits for them, and re-layouts  3.62 us

profile of v5, /device:TPU:0, one launch (start us, length us, event | category | flops | bytes accessed | tf_op | source)
XLA Modules:
  0.0 71.9 jit_solution(14097259693288110058)
XLA Ops:
  0.6 0.0 copy-start
  0.6 0.8 %copy-done = f32[16,8,128]{2,1,0:T(8,128)S(1)} copy-done((f32[16,8,128]{2,1,0:T(8,128)S(1)}, f32[16,8,128]{2,1,0:T(8,128)}, u32[]{:S(2)}) %copy-start) | copy-done | bytes 65560
  1.5 0.0 copy-start.1
  1.5 0.8 %copy-done.1 = f32[16,8,128]{2,1,0:T(8,128)S(1)} copy-done((f32[16,8,128]{2,1,0:T(8,128)S(1)}, f32[16,8,128]{2,1,0:T(8,128)}, u32[]{:S(2)}) %copy-start.1) | copy-done | bytes 65560
  2.3 0.0 copy-start.2
  2.3 0.7 copy-done.2
  3.0 67.6 %shard_map.50 = (f32[16,8,128]{2,1,0:T(8,128)S(1)}, f32[16,8,128]{2,1,0:T(8,128)S(1)}) custom-call(f32[16,8,128]{2,1,0:T(8,128)S(1)} %copy-done, f32[16,8,128]{2,1,0:T(8,128)S(1)} %copy-done.1, s32[2,4,4]{2,1,0:T(4,128)S(1)} %copy-done.2), custom_call_target="tpu_custom_call" | custom-call | tf_op jit(solution)/shard_map/pallas_call | solution.py:458
  70.6 0.6 copy.7
  71.2 0.6 copy.8
Async XLA Ops:
  0.6 0.8 %copy-start = (f32[16,8,128]{2,1,0:T(8,128)S(1)}, f32[16,8,128]{2,1,0:T(8,128)}, u32[]{:S(2)}) copy-start(f32[16,8,128]{2,1,0:T(8,128)} %source_ref.1) | copy-start | bytes 196612
  1.5 0.8 %copy-start.1 = (f32[16,8,128]{2,1,0:T(8,128)S(1)}, f32[16,8,128]{2,1,0:T(8,128)}, u32[]{:S(2)}) copy-start(f32[16,8,128]{2,1,0:T(8,128)} %k_ref.1) | copy-start | bytes 196612
  2.3 0.7 copy-start.2

commit v6 on v5

--- a/solution.py
+++ b/solution.py
@@ -125,9 +125,9 @@
             tx = [wrapped(0, d, sx) for d in range(sx)]
             ty = [wrapped(1, d, sy) for d in range(sy)]
             tz = [wrapped(2, d, sz) for d in range(sz)]
-            for i in range(sx):
-                for j in range(sy):
-                    for k in range(sz):
+            for i in reversed(range(sx)):
+                for j in reversed(range(sy)):
+                    for k in reversed(range(sz)):
                         if i or j or k:
                             body((tx[i], ty[j], tz[k]))
         else:
@@ -360,18 +360,15 @@
                     preferred_element_type=F32)
         rows, columns = iota((GROUPS, GROUPS), 0), iota((GROUPS, GROUPS), 1)
 
-        def eliminate(step, a):
+        a = system
+        for step in range(GROUPS):
             at_row, at_column = rows == step, columns == step
-            row = jnp.sum(jnp.where(at_row, a, 0.0), axis=0, keepdims=True)
-            column = jnp.sum(jnp.where(at_column, a, 0.0), axis=1, keepdims=True)
-            pivot = jnp.sum(jnp.where(at_column, row, 0.0), axis=1, keepdims=True)
-            over = 1.0 / pivot[0:1]
-            swept = a - column * (row * over)
-            swept = jnp.where(at_row, row * over, swept)
-            swept = jnp.where(at_column, column * over, swept)
-            return jnp.where(at_row & at_column, -over, swept)
-
-        return -lax.fori_loop(0, GROUPS, eliminate, system)
+            over = 1.0 / jnp.broadcast_to(a[step : step + 1, step : step + 1], (1, GROUPS))
+            row = a[step : step + 1, :] * over
+            column = jnp.broadcast_to(a[:, step : step + 1], (GROUPS, GROUPS))
+            swept = jnp.where(at_column, column * over, a - column * row)
+            a = jnp.where(at_row, jnp.where(at_column, -over, row), swept)
+        return -a
 
     diagonal = iota((GROUPS, GROUPS), 0) == iota((GROUPS, GROUPS), 1)
 

time: 72.1 us -> 71.7 us (level)
  no operation moved by 1% of the time
where the time goes in v6:
time: 71.7 us; the launch traced here: 71.5 us
  Pallas kernels  67.2 us (94%)
  local copies, waits for them, and re-layouts  3.62 us (5%)
    pallas_call x1, Pallas kernels, on_device(): pl.pallas_call(functools.partial(kernel, sizes), out_shape=[jax.ShapeDtyp...  67.2 us
    unnamed x8, local copies, waits for them, and re-layouts  3.62 us

profile of v6, /device:TPU:0, one launch (start us, length us, event | category | flops | bytes accessed | tf_op | source)
XLA Modules:
  0.0 71.5 jit_solution(13657978569222624029)
XLA Ops:
  0.6 0.0 copy-start
  0.6 0.8 %copy-done = f32[16,8,128]{2,1,0:T(8,128)S(1)} copy-done((f32[16,8,128]{2,1,0:T(8,128)S(1)}, f32[16,8,128]{2,1,0:T(8,128)}, u32[]{:S(2)}) %copy-start) | copy-done | bytes 65560
  1.5 0.0 copy-start.1
  1.5 0.8 %copy-done.1 = f32[16,8,128]{2,1,0:T(8,128)S(1)} copy-done((f32[16,8,128]{2,1,0:T(8,128)S(1)}, f32[16,8,128]{2,1,0:T(8,128)}, u32[]{:S(2)}) %copy-start.1) | copy-done | bytes 65560
  2.3 0.0 copy-start.2
  2.3 0.7 copy-done.2
  3.0 67.2 %shard_map.50 = (f32[16,8,128]{2,1,0:T(8,128)S(1)}, f32[16,8,128]{2,1,0:T(8,128)S(1)}) custom-call(f32[16,8,128]{2,1,0:T(8,128)S(1)} %copy-done, f32[16,8,128]{2,1,0:T(8,128)S(1)} %copy-done.1, s32[2,4,4]{2,1,0:T(4,128)S(1)} %copy-done.2), custom_call_target="tpu_custom_call" | custom-call | tf_op jit(solution)/shard_map/pallas_call | solution.py:455
  70.2 0.6 copy.7
  70.9 0.6 copy.8
Async XLA Ops:
  0.6 0.8 %copy-start = (f32[16,8,128]{2,1,0:T(8,128)S(1)}, f32[16,8,128]{2,1,0:T(8,128)}, u32[]{:S(2)}) copy-start(f32[16,8,128]{2,1,0:T(8,128)} %source_ref.1) | copy-start | bytes 196612
  1.5 0.8 %copy-start.1 = (f32[16,8,128]{2,1,0:T(8,128)S(1)}, f32[16,8,128]{2,1,0:T(8,128)}, u32[]{:S(2)}) copy-start(f32[16,8,128]{2,1,0:T(8,128)} %k_ref.1) | copy-start | bytes 196612
  2.3 0.7 copy-start.2
